TPU v7x, 512 devices: a whole 4x4x16 slice. The times are simulated.
512 devices in a mesh: scen: 16 (over z_hi, y, core), node: 32 (over x, z_lo).
Axes of the slice: x: 4, y: 4, z: 16 (z_hi: 2, z_lo: 8; z = z_hi * 8 + z_lo), core: 2. Of those that a mesh axis runs over, the one named last changes fastest.
Arguments:
- factors: bfloat16 [32, 16, 1024, 1024], P('node', 'scen'), may hold values from -0.1875 to 0.1875
- couple: bfloat16 [32, 16, 1024, 512], P('node', 'scen'), may hold values from -0.1875 to 0.1875
- leaf_rhs: bfloat16 [32, 16, 2, 1024], P('node', 'scen'), may hold values from -6 to 6
- node_diag: float32 [32, 512, 512], P('node', 'scen'), as said below
- node_rhs: float32 [32, 2, 512], P('node', None, 'scen'), may hold values from -6 to 6
- link_root: float32 [32, 512, 512], P('node', 'scen'), may hold values from -1.5 to 1.5
- root_diag: float32 [512, 512], replicated, as said below
- root_rhs: float32 [2, 512], replicated, may hold values from -6 to 6
Outputs:
- leaf_solution: float32 [32, 16, 2, 1024], P('node', 'scen')
- node_solution: float32 [32, 2, 512], P('node', None, 'scen')
- root_solution: float32 [2, 512], replicated
Inputs may be any that keep to these rules, and one draw needn't show every extreme that they name: `node_diag`: symmetric positive definite. `root_diag`: symmetric positive definite.
All inputs are finite; a program needn't handle non-finite values.
Results may differ from a plain program's by a relative error of at most 0.0036.
Values sent between devices are 32-bit elements; how exact they have to be, the bound alone decides.
A program may use at most 64 MiB of HBM per device.

v0:
```python
import jax
import jax.numpy as jnp
from jax import lax
from jax.experimental import pallas as pl
from jax.experimental.pallas import tpu as pltpu
from jax.sharding import Mesh
from jax.sharding import PartitionSpec as P

AXES = ("zh", "y", "core", "x", "zl")
MESH = pl.DeviceIdType.MESH
HIGH = lax.Precision.HIGHEST
F32 = jnp.float32
BF16 = jnp.bfloat16


def dot(a, b, dims=((1,), (0,)), precision=None):
    return lax.dot_general(a, b, (dims, ((), ())), precision=precision, preferred_element_type=F32)


def inverse_128(a, work=()):
    rows = lax.broadcasted_iota(jnp.int32, (8, 128), 0)
    lanes = lax.broadcasted_iota(jnp.int32, (8, 128), 1)
    wide_lanes = lax.broadcasted_iota(jnp.int32, (128, 128), 1)
    work = list(work)
    for s in range(16):
        at = 8 * s
        panel = a[at : at + 8]
        cols = jnp.stack([jnp.broadcast_to(panel[:, at + j : at + j + 1], (8, 128)) for j in range(8)])
        here = (lanes >= at) & (lanes < at + 8)
        panel = jnp.where(here, jnp.where(lanes - at == rows, 1.0, 0.0), panel)
        for j in range(8):
            mine = rows == j
            col = cols[0]
            inv = pl.reciprocal(jnp.broadcast_to(col[j : j + 1], (8, 128)), approx=True)
            f = jnp.where(mine, -inv, col * inv)
            if j < 7:
                rest = cols[1:]
                pivot = jnp.broadcast_to(rest[:, j : j + 1], rest.shape)
                cols = jnp.where(mine[None], 0.0, rest) - f[None] * pivot
            panel = jnp.where(mine, 0.0, panel) - f * jnp.broadcast_to(panel[j : j + 1], (8, 128))
        new = jnp.where((wide_lanes >= at) & (wide_lanes < at + 8), 0.0, a)
        for j in range(8):
            new = new - jnp.broadcast_to(a[:, at + j : at + j + 1], (128, 128)) * jnp.broadcast_to(
                panel[j : j + 1], (128, 128)
            )
        a = jnp.concatenate([part for part in (new[:at], panel, new[at + 8 :]) if part.shape[0]])
        left = 16 - s
        for _ in range(-(-len(work) // left)):
            work.pop(0)()
    for w in work:
        w()
    return a
def inverse_512(a, between=None):
    work = []
    cols = [slice(128 * n, 128 * n + 128) for n in range(4)]
    for k in range(4):
        inv = inverse_128(a[k, :, cols[k]], work)
        if between is not None:
            between(k)
        work = []
        nxt = k + 1
        def row(j, k=k, inv=inv):
            a[k, :, cols[j]] = dot(inv, a[k, :, cols[j]], precision=HIGH)
        def update(i, j, k=k):
            a[i, :, cols[j]] = a[i, :, cols[j]] - dot(a[i, :, cols[k]], a[k, :, cols[j]], precision=HIGH)
        def column(i, k=k, inv=inv):
            a[i, :, cols[k]] = -dot(a[i, :, cols[k]], inv, precision=HIGH)
        others = [n for n in range(4) if n != k]
        if nxt < 4:
            row(nxt); update(nxt, nxt)
        for j in others:
            if j != nxt: work.append(lambda j=j, f=row: f(j))
        for j in others:
            for i in others:
                if not (i == j == nxt): work.append(lambda i=i, j=j, f=update: f(i, j))
        for i in others: work.append(lambda i=i, f=column: f(i))
        def keep(k=k, inv=inv):
            a[k, :, cols[k]] = inv

        work.append(keep)
    for w in work:
        w()


def tile_of(vec):
    return jnp.concatenate([vec[:, 128 * j : 128 * j + 128] for j in range(4)])


def rows_of(tile):
    vec = jnp.concatenate([tile[2 * j : 2 * j + 2] for j in range(4)], axis=1)
    return jnp.concatenate([vec, jnp.zeros((6, 512), F32)])


def body(
    factor_hbm, couple_hbm, rights_hbm, diag_hbm, nrhs_hbm, link_hbm, rdiag_hbm, rrhs_hbm,
    leaf_ref, node_ref, root_ref,
    factor, coupling, rights_ref, diag_ref, nrhs_ref, link_ref, rdiag, rrhs_ref, reduced, projected, part, first, first_from, first_z, first_sum,
    rest, rest_from, rest_z, rest_sum, link, link_t, a, left, e_part, from_x, from_zl, s_all, root, x_rows,
    send, recv, load,
):
    zh, y, core, x, zl = (lax.axis_index(n) for n in AXES)
    scen = zh * 8 + y * 2 + core

    def peer(**at):
        here = dict(zh=zh, y=y, core=core, x=x, zl=zl)
        here.update(at)
        return tuple(here[n] for n in AXES)

    z_peer, core_peer = peer(zh=1 - zh), peer(core=1 - core)
    y_at = [lax.rem(y + d, 4) for d in range(1, 4)]
    x_at = [lax.rem(x + d, 4) for d in range(1, 4)]
    zl_at = [lax.rem(zl + d, 8) for d in range(1, 8)]
    peers = [z_peer, core_peer] + [peer(y=v) for v in y_at] + [peer(x=v) for v in x_at] + [peer(zl=v) for v in zl_at]
    barrier = pltpu.get_barrier_semaphore()
    for device in peers:
        pl.semaphore_signal(barrier, 1, device_id=device, device_id_type=MESH)

    loads = [
        pltpu.make_async_copy(src, dst, load.at[n])
        for n, (src, dst) in enumerate(
            (
                (couple_hbm, coupling),
                (factor_hbm, factor),
                (rights_hbm, rights_ref),
                (diag_hbm, diag_ref),
                (nrhs_hbm, nrhs_ref),
                (link_hbm, link_ref),
                (rdiag_hbm, rdiag),
                (rrhs_hbm, rrhs_ref),
            )
        )
    ]
    for copy in loads:
        copy.start()

    used = [0]

    def start(src, dst, device):
        n = used[0]
        used[0] += 1
        copy = pltpu.make_async_remote_copy(
            src_ref=src, dst_ref=dst, send_sem=send.at[n], recv_sem=recv.at[n], device_id=device, device_id_type=MESH
        )
        copy.start()
        return copy

    for n in range(6):
        loads[n].wait()
    rights = jnp.concatenate([rights_ref[...].astype(F32), jnp.zeros((6, 1024), F32)]).astype(BF16)
    reduced[...] = dot(coupling[...], factor[...], ((0,), (0,))).astype(BF16)
    projected[...] = dot(rights, factor[...])
    for j in range(4):
        part[j, 128 * j :] = dot(reduced[128 * j :], reduced[128 * j : 128 * j + 128], ((1,), (1,)))
    low = projected[...].astype(BF16)
    vec = dot(low, reduced[...], ((1,), (1,)))
    own = pl.ds(pl.multiple_of(32 * scen, 32), 32)
    for j in range(4):
        part[j, own] = part[j, own] + diag_ref[:, 128 * j : 128 * j + 128]
    rows = lax.broadcasted_iota(jnp.int32, (8, 128), 0)
    lanes = lax.broadcasted_iota(jnp.int32, (8, 128), 1)
    strip = jnp.concatenate([nrhs_ref[...]] * 4, axis=1)
    strip = jnp.concatenate([strip] * 4)
    mine = (rows // 2 == scen // 4) & (lanes // 32 == lax.rem(scen, 4))
    vec_tile = tile_of(vec[:2]) + jnp.where(mine, strip, 0.0)
    for c in range(2):
        for v in range(4):
            p = 4 * c + v
            first[c, v] = part[0, 16 * p : 16 * p + 16]
            rest[c, v, 0:48] = part[0, 128 + 48 * p : 176 + 48 * p]
            rest[c, v, 48:96] = part[1, 128 + 48 * p : 176 + 48 * p]
            rest[c, v, 96:128] = part[2, 256 + 32 * p : 288 + 32 * p]
            rest[c, v, 128:144] = part[3, 384 + 16 * p : 400 + 16 * p]
            rest[c, v, 144:152] = vec_tile

    pl.semaphore_wait(barrier, len(peers))

    first_core = start(first.at[1 - core], first_from.at[0], core_peer)
    rest_core = start(rest.at[1 - core], rest_from.at[0], core_peer)
    first_core.wait()
    first[core] = first[core] + first_from[0]
    first_y = [start(first.at[core, v], first_from.at[1, d], peer(y=v)) for d, v in enumerate(y_at)]
    rest_core.wait()
    rest[core] = rest[core] + rest_from[0]
    rest_y = [start(rest.at[core, v], rest_from.at[1, d], peer(y=v)) for d, v in enumerate(y_at)]
    for copy in first_y:
        copy.wait()
    first_z[0] = (first[core, y] + first_from[1, 0]) + (first_from[1, 1] + first_from[1, 2])
    first_far = start(first_z.at[0], first_z.at[1], z_peer)
    for copy in rest_y:
        copy.wait()
    rest_z[0] = (rest[core, y] + rest_from[1, 0]) + (rest_from[1, 1] + rest_from[1, 2])
    rest_far = start(rest_z.at[0], rest_z.at[1], z_peer)

    first_far.wait()
    first_sum[core, y] = first_z[0] + first_z[1]
    first_y = [start(first_sum.at[core, y], first_sum.at[core, y], peer(y=v)) for v in y_at]
    rest_far.wait()
    rest_sum[core, y] = rest_z[0] + rest_z[1]
    rest_y = [start(rest_sum.at[core, y], rest_sum.at[core, y], peer(y=v)) for v in y_at]
    for copy in first_y:
        copy.wait()
    first_core = start(first_sum.at[core], first_sum.at[core], core_peer)
    for copy in rest_y:
        copy.wait()
    rest_core = start(rest_sum.at[core], rest_sum.at[core], core_peer)
    link[own] = link_ref[...]
    link_far = start(link_ref, link.at[own], z_peer)
    link_near = [start(link_ref, link.at[own], peer(y=v)) for v in y_at]
    first_core.wait()
    a[0, :, :128] = jnp.concatenate([first_sum[p // 4, p % 4] for p in range(8)])
    later = {}

    def between(k):
        if k == 0:
            rest_core.wait()
            spans = ((0, 1, 0, 48), (1, 1, 48, 48), (2, 2, 96, 32), (3, 3, 128, 16))
            for j, i0, low_row, n in spans:
                column = jnp.concatenate([rest_sum[p // 4, p % 4, low_row : low_row + n] for p in range(8)])
                for i in range(i0, 4):
                    block = column[128 * (i - i0) : 128 * (i - i0) + 128]
                    a[i, :, 128 * j : 128 * j + 128] = block
                    if i > j:
                        a[j, :, 128 * i : 128 * i + 128] = block.T
        if k == 1:
            link_far.wait()
            for copy in link_near:
                copy.wait()
            far = pl.ds(pl.multiple_of(32 * ((1 - zh) * 8 + y * 2 + core), 32), 32)
            later["near"] = [start(link.at[far], link.at[far], peer(y=v)) for v in y_at]
        if k == 2:
            for copy in later["near"]:
                copy.wait()
            later["core"] = []
            for n in range(8):
                at = pl.ds(pl.multiple_of(32 * (2 * n + core), 32), 32)
                later["core"].append(start(link.at[at], link.at[at], core_peer))

    inverse_512(a, between)
    for copy in later["core"]:
        copy.wait()
    vec_total = rest_sum[core, y, 144:]

    band = pl.ds(pl.multiple_of(128 * y, 128), 128)
    for n in range(4):
        link_t[:, 128 * n : 128 * n + 128] = link[128 * n : 128 * n + 128, band].T
    z_rows = rows_of(vec_total)
    left[:64] = link_t[pl.ds(pl.multiple_of(64 * core, 64), 64)]
    left[64:] = z_rows

    def by_inverse(v):
        out = dot(v[:, :128], a[0], precision=HIGH)
        for n in range(1, 4):
            out = out + dot(v[:, 128 * n : 128 * n + 128], a[n], precision=HIGH)
        return out

    e_rows = dot(by_inverse(left[...]), link[...], precision=HIGH)
    w_tile = tile_of(e_rows[64:66])
    for n in range(4):
        e_part[n, :64] = e_rows[:64, 128 * n : 128 * n + 128]
        e_part[n, 64:] = w_tile

    from_x[x] = e_part[x]
    copies = [start(e_part.at[v], from_x.at[x], peer(x=v)) for v in x_at]
    for copy in copies:
        copy.wait()
    from_zl[zl] = (from_x[0] + from_x[1]) + (from_x[2] + from_x[3])
    copies = [start(from_zl.at[zl], from_zl.at[zl], peer(zl=v)) for v in zl_at]
    for copy in copies:
        copy.wait()
    summed = from_zl[0]
    for n in range(1, 8):
        summed = summed + from_zl[n]
    s_all[core, y, x] = summed[:64]
    w_sum = rows_of(summed[64:])
    copies = [start(s_all.at[core, y, x], s_all.at[core, y, x], peer(x=v)) for v in x_at]
    for copy in copies:
        copy.wait()
    copies = [start(s_all.at[core, y], s_all.at[core, y], peer(y=v)) for v in y_at]
    for copy in copies:
        copy.wait()
    copy = start(s_all.at[core], s_all.at[core], core_peer)
    loads[6].wait()
    loads[7].wait()
    copy.wait()
    for i in range(4):
        for c in range(2):
            at = slice(64 * c, 64 * c + 64)
            for n in range(4):
                cols = slice(128 * n, 128 * n + 128)
                root[i, at, cols] = s_all[c, i, n] + rdiag[128 * i + 64 * c : 128 * i + 64 * c + 64, cols]
    inverse_512(root)
    q_rows = jnp.concatenate([rrhs_ref[...], jnp.zeros((6, 512), F32)])
    v = w_sum - q_rows
    root_sol = dot(v[:, :128], root[0], precision=HIGH)
    for n in range(1, 4):
        root_sol = root_sol + dot(v[:, 128 * n : 128 * n + 128], root[n], precision=HIGH)
    root_ref[...] = root_sol[:2]
    shifted = z_rows - dot(root_sol, link[...], ((1,), (1,)), precision=HIGH)
    node_sol = by_inverse(shifted)
    for n in range(16):
        x_rows[n] = node_sol[:2, 32 * n : 32 * n + 32]
    node_ref[...] = x_rows[scen]
    update = dot(node_sol.astype(BF16), reduced[...])
    difference = (update - projected[...]).astype(BF16)
    leaf_ref[...] = dot(difference, factor[...], ((1,), (1,)))[:2]


def local(factors, couple, leaf_rhs, node_diag, node_rhs, link_root, root_diag, root_rhs):
    vmem, hbm = pl.BlockSpec(memory_space=pltpu.VMEM), pl.BlockSpec(memory_space=pl.ANY)
    copies = 64
    leaf, node, root = pl.pallas_call(
        body,
        out_shape=(
            jax.ShapeDtypeStruct((2, 1024), F32),
            jax.ShapeDtypeStruct((2, 32), F32),
            jax.ShapeDtypeStruct((2, 512), F32),
        ),
        in_specs=[hbm] * 8,
        out_specs=(vmem, vmem, vmem),
        scratch_shapes=[
            pltpu.VMEM((1024, 1024), BF16),
            pltpu.VMEM((1024, 512), BF16),
            pltpu.VMEM((2, 1024), BF16),
            pltpu.VMEM((32, 512), F32),
            pltpu.VMEM((2, 32), F32),
            pltpu.VMEM((32, 512), F32),
            pltpu.VMEM((512, 512), F32),
            pltpu.VMEM((2, 512), F32),
            pltpu.VMEM((512, 1024), BF16),
            pltpu.VMEM((8, 1024), F32),
            pltpu.VMEM((4, 512, 128), F32),
            pltpu.VMEM((2, 4, 16, 128), F32),
            pltpu.VMEM((2, 4, 16, 128), F32),
            pltpu.VMEM((2, 16, 128), F32),
            pltpu.VMEM((2, 4, 16, 128), F32),
            pltpu.VMEM((2, 4, 152, 128), F32),
            pltpu.VMEM((2, 4, 152, 128), F32),
            pltpu.VMEM((2, 152, 128), F32),
            pltpu.VMEM((2, 4, 152, 128), F32),
            pltpu.VMEM((512, 512), F32),
            pltpu.VMEM((128, 512), F32),
            pltpu.VMEM((4, 128, 512), F32),
            pltpu.VMEM((72, 512), F32),
            pltpu.VMEM((4, 72, 128), F32),
            pltpu.VMEM((4, 72, 128), F32),
            pltpu.VMEM((8, 72, 128), F32),
            pltpu.VMEM((2, 4, 4, 64, 128), F32),
            pltpu.VMEM((4, 128, 512), F32),
            pltpu.VMEM((16, 2, 32), F32),
            pltpu.SemaphoreType.DMA((copies,)),
            pltpu.SemaphoreType.DMA((copies,)),
            pltpu.SemaphoreType.DMA((8,)),
        ],
        compiler_params=pltpu.CompilerParams(
            collective_id=0, has_side_effects=True, vmem_limit_bytes=60 * 1024 * 1024
        ),
        name="newton",
    )(factors[0, 0], couple[0, 0], leaf_rhs[0, 0], node_diag[0], node_rhs[0], link_root[0], root_diag, root_rhs)
    return (leaf[None, None], node[None], root)


def solution(mesh):
    torus = Mesh(mesh.devices.reshape(2, 4, 2, 4, 8), AXES)
    scen, node = ("zh", "y", "core"), ("x", "zl")
    placed = (
        P(node, scen, None, None),
        P(node, scen, None, None),
        P(node, scen, None, None),
        P(node, scen, None),
        P(node, None, scen),
        P(node, scen, None),
        P(),
        P(),
    )
    return jax.shard_map(
        local,
        mesh=torus,
        in_specs=placed,
        out_specs=(P(node, scen, None, None), P(node, None, scen), P()),
        check_vma=False,
    )
```

profile of v0, /device:TPU:1, one launch (start us, length us, event | category | flops | bytes accessed | tf_op | source)
XLA Modules:
  0.0 120.0 jit_solution(16072405205824652531)
XLA Ops:
  0.6 115.5 %newton.1 = (f32[2,1024]{1,0:T(2,128)}, f32[2,32]{1,0:T(2,128)}, f32[2,512]{1,0:T(2,128)}) custom-call(bf16[1024,1024]{1,0:T(8,128)(2,1)} %bitcast.8, bf16[1024,512]{1,0:T(8,128)(2,1)} %bitcast.9, bf16[2,1024]{1,0:T(2,128)(2,1)} %bitcast.13, f32[32,512]{1,0:T(8,128)} %bitcast.10, f32[2,32]{1,0:T(2,128)} %bitcast.14, f32[32,512]{1,0:T(8,128)} %bitcast.11, ...), custom_call_target="tpu_custom_call" | custom-call | tf_op jit(solution)/shard_map/newton/pallas_call | solution.py:311
  116.2 1.3 %copy.14 = f32[1,1,2,1024]{3,2,1,0:T(2,128)} copy(f32[1,1,2,1024]{3,2,1,0:T(2,128)} %bitcast.12) | data formatting | bytes 16384
  117.5 1.2 %copy.15 = f32[1,2,32]{2,1,0:T(2,128)} copy(f32[1,2,32]{2,1,0:T(2,128)} %bitcast.15) | data formatting | bytes 512
  118.7 1.3 %copy.16 = f32[2,512]{1,0:T(2,128)} copy(f32[2,512]{1,0:T(2,128)} %get-tuple-element.14) | data formatting | bytes 8192
where the time goes:
time: 121 us; the launch traced here: 120 us
  Pallas kernels  116 us (96%)
  local copies, waits for them, and re-layouts  3.79 us (3%)
    pallas_call x1, Pallas kernels, local(): pl.pallas_call(body, out_shape=(jax.ShapeDtypeStruct((2, 1024), F32), jax...  116 us
    unnamed x3, local copies, waits for them, and re-layouts  3.79 us

commit v1 on v0

--- a/solution.py
+++ b/solution.py
@@ -17,14 +17,22 @@
     return lax.dot_general(a, b, (dims, ((), ())), precision=precision, preferred_element_type=F32)
 
 
+def thirds(v):
+    high = v.astype(BF16).astype(F32)
+    mid = (v - high).astype(BF16).astype(F32)
+    return high, mid, v - high - mid
+
+
 def inverse_128(a, work=()):
     rows = lax.broadcasted_iota(jnp.int32, (8, 128), 0)
     lanes = lax.broadcasted_iota(jnp.int32, (8, 128), 1)
     wide_lanes = lax.broadcasted_iota(jnp.int32, (128, 128), 1)
     work = list(work)
+    following = a[:8]
     for s in range(16):
         at = 8 * s
-        panel = a[at : at + 8]
+        panel = following
+        ah, am, al = thirds(jnp.where(lanes < at, -panel, panel))
         cols = jnp.stack([jnp.broadcast_to(panel[:, at + j : at + j + 1], (8, 128)) for j in range(8)])
         here = (lanes >= at) & (lanes < at + 8)
         panel = jnp.where(here, jnp.where(lanes - at == rows, 1.0, 0.0), panel)
@@ -38,18 +46,23 @@
                 pivot = jnp.broadcast_to(rest[:, j : j + 1], rest.shape)
                 cols = jnp.where(mine[None], 0.0, rest) - f[None] * pivot
             panel = jnp.where(mine, 0.0, panel) - f * jnp.broadcast_to(panel[j : j + 1], (8, 128))
-        new = jnp.where((wide_lanes >= at) & (wide_lanes < at + 8), 0.0, a)
-        for j in range(8):
-            new = new - jnp.broadcast_to(a[:, at + j : at + j + 1], (128, 128)) * jnp.broadcast_to(
-                panel[j : j + 1], (128, 128)
-            )
+        if s < 15:
+            old = a[at + 8 : at + 16]
+            following = jnp.where(here, 0.0, old)
+            for j in range(8):
+                following = following - jnp.broadcast_to(old[:, at + j : at + j + 1], (8, 128)) * jnp.broadcast_to(
+                    panel[j : j + 1], (8, 128)
+                )
+        bh, bm, bl = thirds(panel)
+        left = jnp.concatenate([ah, ah, ah, am, am, al]).astype(BF16)
+        right = jnp.concatenate([bh, bm, bl, bh, bm, bh]).astype(BF16)
+        new = jnp.where((wide_lanes >= at) & (wide_lanes < at + 8), 0.0, a) - dot(left, right, ((0,), (0,)))
         a = jnp.concatenate([part for part in (new[:at], panel, new[at + 8 :]) if part.shape[0]])
-        left = 16 - s
-        for _ in range(-(-len(work) // left)):
+        for _ in range(-(-len(work) // (16 - s))):
             work.pop(0)()
-    for w in work:
-        w()
     return a
+
+
 def inverse_512(a, between=None):
     work = []
     cols = [slice(128 * n, 128 * n + 128) for n in range(4)]
@@ -93,9 +106,9 @@
 
 def body(
     factor_hbm, couple_hbm, rights_hbm, diag_hbm, nrhs_hbm, link_hbm, rdiag_hbm, rrhs_hbm,
-    leaf_ref, node_ref, root_ref,
+    out_ref,
     factor, coupling, rights_ref, diag_ref, nrhs_ref, link_ref, rdiag, rrhs_ref, reduced, projected, part, first, first_from, first_z, first_sum,
-    rest, rest_from, rest_z, rest_sum, link, link_t, a, left, e_part, from_x, from_zl, s_all, root, x_rows,
+    rest, rest_from, rest_z, rest_sum, link, link_t, a, left, e_part, from_x, from_zl, back, s_all, root, x_rows,
     send, recv, load,
 ):
     zh, y, core, x, zl = (lax.axis_index(n) for n in AXES)
@@ -253,7 +266,8 @@
             out = out + dot(v[:, 128 * n : 128 * n + 128], a[n], precision=HIGH)
         return out
 
-    e_rows = dot(by_inverse(left[...]), link[...], precision=HIGH)
+    solved = by_inverse(left[...])
+    e_rows = dot(solved, link[...], precision=HIGH)
     w_tile = tile_of(e_rows[64:66])
     for n in range(4):
         e_part[n, :64] = e_rows[:64, 128 * n : 128 * n + 128]
@@ -265,6 +279,8 @@
         copy.wait()
     from_zl[zl] = (from_x[0] + from_x[1]) + (from_x[2] + from_x[3])
     copies = [start(from_zl.at[zl], from_zl.at[zl], peer(zl=v)) for v in zl_at]
+    for n in range(4):
+        back[128 * n : 128 * n + 128] = dot(a[n], link[...], precision=HIGH)
     for copy in copies:
         copy.wait()
     summed = from_zl[0]
@@ -294,29 +310,30 @@
     root_sol = dot(v[:, :128], root[0], precision=HIGH)
     for n in range(1, 4):
         root_sol = root_sol + dot(v[:, 128 * n : 128 * n + 128], root[n], precision=HIGH)
-    root_ref[...] = root_sol[:2]
-    shifted = z_rows - dot(root_sol, link[...], ((1,), (1,)), precision=HIGH)
-    node_sol = by_inverse(shifted)
+    node_sol = solved[64:] - dot(root_sol, back[...], ((1,), (1,)), precision=HIGH)
     for n in range(16):
         x_rows[n] = node_sol[:2, 32 * n : 32 * n + 32]
-    node_ref[...] = x_rows[scen]
     update = dot(node_sol.astype(BF16), reduced[...])
     difference = (update - projected[...]).astype(BF16)
-    leaf_ref[...] = dot(difference, factor[...], ((1,), (1,)))[:2]
+    out_ref[0:2] = dot(difference, factor[...], ((1,), (1,)))[:2]
+    out_ref[2:4, :512] = root_sol[:2]
+    out_ref[4:6, :32] = x_rows[scen]
+
+
+def parted(all_ref, leaf_ref, node_ref, root_ref):
+    leaf_ref[...] = all_ref[0:2]
+    root_ref[...] = all_ref[2:4, :512]
+    node_ref[...] = all_ref[4:6, :32]
 
 
 def local(factors, couple, leaf_rhs, node_diag, node_rhs, link_root, root_diag, root_rhs):
     vmem, hbm = pl.BlockSpec(memory_space=pltpu.VMEM), pl.BlockSpec(memory_space=pl.ANY)
     copies = 64
-    leaf, node, root = pl.pallas_call(
+    everything = pl.pallas_call(
         body,
-        out_shape=(
-            jax.ShapeDtypeStruct((2, 1024), F32),
-            jax.ShapeDtypeStruct((2, 32), F32),
-            jax.ShapeDtypeStruct((2, 512), F32),
-        ),
+        out_shape=jax.ShapeDtypeStruct((8, 1024), F32),
         in_specs=[hbm] * 8,
-        out_specs=(vmem, vmem, vmem),
+        out_specs=vmem,
         scratch_shapes=[
             pltpu.VMEM((1024, 1024), BF16),
             pltpu.VMEM((1024, 512), BF16),
@@ -344,6 +361,7 @@
             pltpu.VMEM((4, 72, 128), F32),
             pltpu.VMEM((4, 72, 128), F32),
             pltpu.VMEM((8, 72, 128), F32),
+            pltpu.VMEM((512, 512), F32),
             pltpu.VMEM((2, 4, 4, 64, 128), F32),
             pltpu.VMEM((4, 128, 512), F32),
             pltpu.VMEM((16, 2, 32), F32),
@@ -356,6 +374,17 @@
         ),
         name="newton",
     )(factors[0, 0], couple[0, 0], leaf_rhs[0, 0], node_diag[0], node_rhs[0], link_root[0], root_diag, root_rhs)
+    leaf, node, root = pl.pallas_call(
+        parted,
+        out_shape=(
+            jax.ShapeDtypeStruct((2, 1024), F32),
+            jax.ShapeDtypeStruct((2, 32), F32),
+            jax.ShapeDtypeStruct((2, 512), F32),
+        ),
+        in_specs=[vmem],
+        out_specs=(vmem, vmem, vmem),
+        name="parted",
+    )(everything)
     return (leaf[None, None], node[None], root)
 
 

time: 121 us -> 115 us (0.950)
  local copies, waits for them, and re-layouts: 3.79 us -> 0 us
  Pallas kernels: 116 us -> 114 us
    unnamed x3 -> x0, local copies, waits for them, and re-layouts: 3.79 us -> none
    pallas_call x1 -> x2, Pallas kernels: 116 us -> 114 us  [the longest x1 113 us: local(): pl.pallas_call(body, out_shape=jax.ShapeDtypeStruct((8, 1024), F32), in_s...]
where the time goes in v1:
time: 115 us
  Pallas kernels  114 us (99%)
    pallas_call x1, Pallas kernels, local(): pl.pallas_call(body, out_shape=jax.ShapeDtypeStruct((8, 1024), F32), in_s...  113 us

profile of v1, /device:TPU:1, one launch (start us, length us, event | category | flops | bytes accessed | tf_op | source)
XLA Modules:
  0.0 114.6 jit_solution(3707723825410935516)
XLA Ops:
  0.6 112.6 %newton.1.all_ref = f32[8,1024]{1,0:T(8,128)} custom-call(bf16[1024,1024]{1,0:T(8,128)(2,1)} %bitcast.8, bf16[1024,512]{1,0:T(8,128)(2,1)} %bitcast.9, bf16[2,1024]{1,0:T(2,128)(2,1)} %bitcast.12, f32[32,512]{1,0:T(8,128)} %bitcast.10, f32[2,32]{1,0:T(2,128)} %bitcast.13, f32[32,512]{1,0:T(8,128)} %bitcast.11, f32[512,512]{1,0:T(8,128)} %rdiag_hbm.1, ...), custom_call_target="tpu_custom_call" | custom-call | tf_op jit(solution)/shard_map/newton/pallas_call | solution.py:332
  113.2 1.4 %parted.1 = (f32[2,1024]{1,0:T(2,128)}, f32[2,32]{1,0:T(2,128)}, f32[2,512]{1,0:T(2,128)}) custom-call(f32[8,1024]{1,0:T(8,128)} %newton.1.all_ref), custom_call_target="tpu_custom_call" | custom-call | tf_op jit(solution)/shard_map/parted/pallas_call | solution.py:377

commit v2 on v1

--- a/solution.py
+++ b/solution.py
@@ -108,7 +108,7 @@
     factor_hbm, couple_hbm, rights_hbm, diag_hbm, nrhs_hbm, link_hbm, rdiag_hbm, rrhs_hbm,
     out_ref,
     factor, coupling, rights_ref, diag_ref, nrhs_ref, link_ref, rdiag, rrhs_ref, reduced, projected, part, first, first_from, first_z, first_sum,
-    rest, rest_from, rest_z, rest_sum, link, link_t, a, left, e_part, from_x, from_zl, back, s_all, root, x_rows,
+    rest, rest_from, rest_z, rest_sum, link, link_t, a, left, e_blocks, e_part, from_x, from_zl, back, s_all, root, v_blocks, x_blocks, x_rows,
     send, recv, load,
 ):
     zh, y, core, x, zl = (lax.axis_index(n) for n in AXES)
@@ -270,8 +270,13 @@
     e_rows = dot(solved, link[...], precision=HIGH)
     w_tile = tile_of(e_rows[64:66])
     for n in range(4):
-        e_part[n, :64] = e_rows[:64, 128 * n : 128 * n + 128]
-        e_part[n, 64:] = w_tile
+        e_blocks[n] = e_rows[:64, 128 * n : 128 * n + 128]
+    for q in range(3):
+        block = e_blocks[lax.rem(y + q, 4)]
+        for n in range(4):
+            e_part[n, 16 * q : 16 * q + 16] = block[16 * n : 16 * n + 16]
+    for n in range(4):
+        e_part[n, 48:] = w_tile
 
     from_x[x] = e_part[x]
     copies = [start(e_part.at[v], from_x.at[x], peer(x=v)) for v in x_at]
@@ -286,30 +291,54 @@
     summed = from_zl[0]
     for n in range(1, 8):
         summed = summed + from_zl[n]
-    s_all[core, y, x] = summed[:64]
-    w_sum = rows_of(summed[64:])
+    s_all[core, y, x] = summed[:48]
+    w_sum = rows_of(summed[48:])
     copies = [start(s_all.at[core, y, x], s_all.at[core, y, x], peer(x=v)) for v in x_at]
+    for n in (6, 7):
+        loads[n].wait()
+    v = w_sum - jnp.concatenate([rrhs_ref[...], jnp.zeros((6, 512), F32)])
+    for n in range(4):
+        v_blocks[n] = v[:, 128 * n : 128 * n + 128]
     for copy in copies:
         copy.wait()
-    copies = [start(s_all.at[core, y], s_all.at[core, y], peer(y=v)) for v in y_at]
-    for copy in copies:
-        copy.wait()
-    copy = start(s_all.at[core], s_all.at[core], core_peer)
-    loads[6].wait()
-    loads[7].wait()
-    copy.wait()
-    for i in range(4):
-        for c in range(2):
-            at = slice(64 * c, 64 * c + 64)
-            for n in range(4):
-                cols = slice(128 * n, 128 * n + 128)
-                root[i, at, cols] = s_all[c, i, n] + rdiag[128 * i + 64 * c : 128 * i + 64 * c + 64, cols]
-    inverse_512(root)
-    q_rows = jnp.concatenate([rrhs_ref[...], jnp.zeros((6, 512), F32)])
-    v = w_sum - q_rows
-    root_sol = dot(v[:, :128], root[0], precision=HIGH)
-    for n in range(1, 4):
-        root_sol = root_sol + dot(v[:, 128 * n : 128 * n + 128], root[n], precision=HIGH)
+    own_block = start(s_all.at[core, y], s_all.at[core, y], core_peer)
+    other_blocks = [start(s_all.at[core, y], s_all.at[core, y], peer(y=v)) for v in y_at]
+
+    turn = [y] + y_at
+
+    def spot(t):
+        return pl.ds(pl.multiple_of(128 * turn[t % 4], 128), 128)
+
+    def place(t, q):
+        block = jnp.concatenate([s_all[n // 4, turn[t], n % 4, 16 * q : 16 * q + 16] for n in range(8)])
+        u = (t + q) % 4
+        root[t, :, 128 * u : 128 * u + 128] = block + rdiag[spot(t), spot(u)]
+        if q == 1:
+            root[u, :, 128 * t : 128 * t + 128] = block.T + rdiag[spot(u), spot(t)]
+
+    def between_root(k):
+        if k == 0:
+            forward = []
+            for copy, v in zip(other_blocks, reversed(y_at)):
+                copy.wait()
+                forward.append(start(s_all.at[core, v], s_all.at[core, v], core_peer))
+            place(0, 1)
+            place(0, 2)
+            for copy in forward:
+                copy.wait()
+            for t in range(1, 4):
+                for q in range(3):
+                    place(t, q)
+
+    own_block.wait()
+    place(0, 0)
+    inverse_512(root, between_root)
+    turned = dot(v_blocks[turn[0]], root[0], precision=HIGH)
+    for t in range(1, 4):
+        turned = turned + dot(v_blocks[turn[t]], root[t], precision=HIGH)
+    for t in range(4):
+        x_blocks[turn[t]] = turned[:, 128 * t : 128 * t + 128]
+    root_sol = jnp.concatenate([x_blocks[n] for n in range(4)], axis=1)
     node_sol = solved[64:] - dot(root_sol, back[...], ((1,), (1,)), precision=HIGH)
     for n in range(16):
         x_rows[n] = node_sol[:2, 32 * n : 32 * n + 32]
@@ -358,12 +387,15 @@
             pltpu.VMEM((128, 512), F32),
             pltpu.VMEM((4, 128, 512), F32),
             pltpu.VMEM((72, 512), F32),
-            pltpu.VMEM((4, 72, 128), F32),
-            pltpu.VMEM((4, 72, 128), F32),
-            pltpu.VMEM((8, 72, 128), F32),
+            pltpu.VMEM((4, 64, 128), F32),
+            pltpu.VMEM((4, 56, 128), F32),
+            pltpu.VMEM((4, 56, 128), F32),
+            pltpu.VMEM((8, 56, 128), F32),
             pltpu.VMEM((512, 512), F32),
-            pltpu.VMEM((2, 4, 4, 64, 128), F32),
+            pltpu.VMEM((2, 4, 4, 48, 128), F32),
             pltpu.VMEM((4, 128, 512), F32),
+            pltpu.VMEM((4, 8, 128), F32),
+            pltpu.VMEM((4, 8, 128), F32),
             pltpu.VMEM((16, 2, 32), F32),
             pltpu.SemaphoreType.DMA((copies,)),
             pltpu.SemaphoreType.DMA((copies,)),

time: 115 us -> 109 us (0.948)
  Pallas kernels: 114 us -> 108 us
    pallas_call x1, Pallas kernels: 113 us -> 107 us  [local(): pl.pallas_call(body, out_shape=jax.ShapeDtypeStruct((8, 1024), F32), in_s...]
where the time goes in v2:
time: 109 us
  Pallas kernels  108 us (99%)
    pallas_call x1, Pallas kernels, local(): pl.pallas_call(body, out_shape=jax.ShapeDtypeStruct((8, 1024), F32), in_s...  107 us

profile of v2, /device:TPU:1, one launch (start us, length us, event | category | flops | bytes accessed | tf_op | source)
XLA Modules:
  0.0 108.5 jit_solution(2395843106893261508)
XLA Ops:
  0.6 106.5 %newton.1.all_ref = f32[8,1024]{1,0:T(8,128)} custom-call(bf16[1024,1024]{1,0:T(8,128)(2,1)} %bitcast.8, bf16[1024,512]{1,0:T(8,128)(2,1)} %bitcast.9, bf16[2,1024]{1,0:T(2,128)(2,1)} %bitcast.12, f32[32,512]{1,0:T(8,128)} %bitcast.10, f32[2,32]{1,0:T(2,128)} %bitcast.13, f32[32,512]{1,0:T(8,128)} %bitcast.11, f32[512,512]{1,0:T(8,128)} %rdiag_hbm.1, ...), custom_call_target="tpu_custom_call" | custom-call | tf_op jit(solution)/shard_map/newton/pallas_call | solution.py:361
  107.2 1.4 %parted.1 = (f32[2,1024]{1,0:T(2,128)}, f32[2,32]{1,0:T(2,128)}, f32[2,512]{1,0:T(2,128)}) custom-call(f32[8,1024]{1,0:T(8,128)} %newton.1.all_ref), custom_call_target="tpu_custom_call" | custom-call | tf_op jit(solution)/shard_map/parted/pallas_call | solution.py:409

commit v3 on v2

--- a/solution.py
+++ b/solution.py
@@ -207,25 +207,27 @@
     first_far.wait()
     first_sum[core, y] = first_z[0] + first_z[1]
     first_y = [start(first_sum.at[core, y], first_sum.at[core, y], peer(y=v)) for v in y_at]
+    for copy in first_y:
+        copy.wait()
+    first_core = start(first_sum.at[core], first_sum.at[core], core_peer)
     rest_far.wait()
     rest_sum[core, y] = rest_z[0] + rest_z[1]
     rest_y = [start(rest_sum.at[core, y], rest_sum.at[core, y], peer(y=v)) for v in y_at]
-    for copy in first_y:
-        copy.wait()
-    first_core = start(first_sum.at[core], first_sum.at[core], core_peer)
-    for copy in rest_y:
-        copy.wait()
-    rest_core = start(rest_sum.at[core], rest_sum.at[core], core_peer)
+    rest_core = [start(rest_sum.at[core, y], rest_sum.at[core, y], core_peer)]
     link[own] = link_ref[...]
     link_far = start(link_ref, link.at[own], z_peer)
-    link_near = [start(link_ref, link.at[own], peer(y=v)) for v in y_at]
     first_core.wait()
     a[0, :, :128] = jnp.concatenate([first_sum[p // 4, p % 4] for p in range(8)])
     later = {}
 
     def between(k):
         if k == 0:
-            rest_core.wait()
+            for copy, v in zip(rest_y, reversed(y_at)):
+                copy.wait()
+                rest_core.append(start(rest_sum.at[core, v], rest_sum.at[core, v], core_peer))
+            later["own"] = [start(link_ref, link.at[own], peer(y=v)) for v in y_at]
+            for copy in rest_core:
+                copy.wait()
             spans = ((0, 1, 0, 48), (1, 1, 48, 48), (2, 2, 96, 32), (3, 3, 128, 16))
             for j, i0, low_row, n in spans:
                 column = jnp.concatenate([rest_sum[p // 4, p % 4, low_row : low_row + n] for p in range(8)])
@@ -236,7 +238,7 @@
                         a[j, :, 128 * i : 128 * i + 128] = block.T
         if k == 1:
             link_far.wait()
-            for copy in link_near:
+            for copy in later["own"]:
                 copy.wait()
             far = pl.ds(pl.multiple_of(32 * ((1 - zh) * 8 + y * 2 + core), 32), 32)
             later["near"] = [start(link.at[far], link.at[far], peer(y=v)) for v in y_at]

time: 109 us -> 103 us (0.945)
  Pallas kernels: 108 us -> 102 us
    pallas_call x1, Pallas kernels: 107 us -> 101 us  [local(): pl.pallas_call(body, out_shape=jax.ShapeDtypeStruct((8, 1024), F32), in_s...]
where the time goes in v3:
time: 103 us
  Pallas kernels  102 us (99%)
    pallas_call x1, Pallas kernels, local(): pl.pallas_call(body, out_shape=jax.ShapeDtypeStruct((8, 1024), F32), in_s...  101 us

profile of v3, /device:TPU:1, one launch (start us, length us, event | category | flops | bytes accessed | tf_op | source)
XLA Modules:
  0.0 102.9 jit_solution(564390580477407913)
XLA Ops:
  0.6 100.9 %newton.1.all_ref = f32[8,1024]{1,0:T(8,128)} custom-call(bf16[1024,1024]{1,0:T(8,128)(2,1)} %bitcast.8, bf16[1024,512]{1,0:T(8,128)(2,1)} %bitcast.9, bf16[2,1024]{1,0:T(2,128)(2,1)} %bitcast.12, f32[32,512]{1,0:T(8,128)} %bitcast.10, f32[2,32]{1,0:T(2,128)} %bitcast.13, f32[32,512]{1,0:T(8,128)} %bitcast.11, f32[512,512]{1,0:T(8,128)} %rdiag_hbm.1, ...), custom_call_target="tpu_custom_call" | custom-call | tf_op jit(solution)/shard_map/newton/pallas_call | solution.py:363
  101.5 1.4 %parted.1 = (f32[2,1024]{1,0:T(2,128)}, f32[2,32]{1,0:T(2,128)}, f32[2,512]{1,0:T(2,128)}) custom-call(f32[8,1024]{1,0:T(8,128)} %newton.1.all_ref), custom_call_target="tpu_custom_call" | custom-call | tf_op jit(solution)/shard_map/parted/pallas_call | solution.py:411

commit v4 on v3

--- a/solution.py
+++ b/solution.py
@@ -63,13 +63,15 @@
     return a
 
 
-def inverse_512(a, between=None):
+def inverse_512(a, between=None, finish=True):
     work = []
     cols = [slice(128 * n, 128 * n + 128) for n in range(4)]
     for k in range(4):
         inv = inverse_128(a[k, :, cols[k]], work)
         if between is not None:
             between(k)
+        if k == 3 and not finish:
+            return inv
         work = []
         nxt = k + 1
         def row(j, k=k, inv=inv):
@@ -334,10 +336,12 @@
 
     own_block.wait()
     place(0, 0)
-    inverse_512(root, between_root)
+    last = inverse_512(root, between_root, finish=False)
     turned = dot(v_blocks[turn[0]], root[0], precision=HIGH)
-    for t in range(1, 4):
+    for t in range(1, 3):
         turned = turned + dot(v_blocks[turn[t]], root[t], precision=HIGH)
+    x_last = dot(v_blocks[turn[3]] - turned[:, 384:], last, precision=HIGH)
+    turned = jnp.concatenate([turned[:, :384] + dot(x_last, root[3, :, :384], precision=HIGH), x_last], axis=1)
     for t in range(4):
         x_blocks[turn[t]] = turned[:, 128 * t : 128 * t + 128]
     root_sol = jnp.concatenate([x_blocks[n] for n in range(4)], axis=1)

time: 103 us -> 102 us (level)
    pallas_call x1, Pallas kernels: 101 us -> 99.7 us  [local(): pl.pallas_call(body, out_shape=jax.ShapeDtypeStruct((8, 1024), F32), in_s...]
where the time goes in v4:
time: 102 us
  Pallas kernels  101 us (99%)
    pallas_call x1, Pallas kernels, local(): pl.pallas_call(body, out_shape=jax.ShapeDtypeStruct((8, 1024), F32), in_s...  99.7 us

profile of v4, /device:TPU:1, one launch (start us, length us, event | category | flops | bytes accessed | tf_op | source)
XLA Modules:
  0.0 101.7 jit_solution(8323049902792967115)
XLA Ops:
  0.6 99.7 %newton.1.all_ref = f32[8,1024]{1,0:T(8,128)} custom-call(bf16[1024,1024]{1,0:T(8,128)(2,1)} %bitcast.8, bf16[1024,512]{1,0:T(8,128)(2,1)} %bitcast.9, bf16[2,1024]{1,0:T(2,128)(2,1)} %bitcast.12, f32[32,512]{1,0:T(8,128)} %bitcast.10, f32[2,32]{1,0:T(2,128)} %bitcast.13, f32[32,512]{1,0:T(8,128)} %bitcast.11, f32[512,512]{1,0:T(8,128)} %rdiag_hbm.1, ...), custom_call_target="tpu_custom_call" | custom-call | tf_op jit(solution)/shard_map/newton/pallas_call | solution.py:367
  100.3 1.4 %parted.1 = (f32[2,1024]{1,0:T(2,128)}, f32[2,32]{1,0:T(2,128)}, f32[2,512]{1,0:T(2,128)}) custom-call(f32[8,1024]{1,0:T(8,128)} %newton.1.all_ref), custom_call_target="tpu_custom_call" | custom-call | tf_op jit(solution)/shard_map/parted/pallas_call | solution.py:415
